TPU v7x, 32 devices: a whole 2x2x4 slice. The times are simulated.
32 devices in a mesh: groups: 2 (over y), tile: 4 (over x, core), tm: 4 (over z).
Axes of the slice: x: 2, y: 2, z: 4, core: 2. Of those that a mesh axis runs over, the one named last changes fastest.
Arguments:
- frames: float32 [2048, 8192], P(('groups', 'tm'), 'tile'), parts along dimension 0
- segment_ids: int32 [2048], P(('groups', 'tm')), parts along dimension 0, may hold values from 0 to 7, never falling along the last dimension, each value on 1 to 512 neighbouring positions
Outputs:
- instant_cov: float32 [16384, 8192], P(('groups', 'tile'), 'tm'), parts along dimension 0
- lagged_cov: float32 [16384, 8192], P(('groups', 'tile'), 'tm'), parts along dimension 0
There are 2 independent parts, one for each index of `groups`. A program takes and returns all parts, laid end to end along the dimension named above; each array names one. Nothing has to cross between parts.
Inputs may be any that keep to these rules, and one draw needn't show every extreme that they name: `segment_ids`: never falling along the frames; each segment has at most 512 frames, and one has exactly that many.
All inputs are finite; a program needn't handle non-finite values.
Results may differ from a plain program's by a relative error of at most 0.0021.
Values may be sent and summed in bfloat16 or wider, within the bound.
A program may use at most 128 MiB of HBM per device.

v0:
```python
import jax
import jax.numpy as jnp
from jax import lax
from jax.sharding import PartitionSpec as P

LAG = 100


def from_behind(value, axis, steps):
    count = lax.axis_size(axis)
    initial, last = (max(0, -steps), min(count, count - steps))
    return lax.ppermute(value, axis, [(source, source + steps) for source in range(initial, last)])


def broadcast(x, axis, root):
    mine = lax.axis_index(axis) == root
    return lax.psum(jnp.where(mine, x, jnp.zeros_like(x)), axis)


def body(frames, segment_ids):
    slab_rows = frames.shape[0]
    ahead_rows, ahead_seg = from_behind((frames[:LAG], segment_ids[:LAG]), "tm", -1)
    later = jnp.concatenate([frames, ahead_rows], axis=0)[LAG:]
    later_seg = jnp.concatenate([segment_ids, ahead_seg], axis=0)[LAG:]
    places = lax.axis_index("tm") * slab_rows + jnp.arange(slab_rows, dtype=jnp.int32)
    total_frames = slab_rows * lax.axis_size("tm")
    weight = ((segment_ids == later_seg) & (places + LAG < total_frames)).astype(jnp.float32)
    local_sums = jnp.sum(weight[:, None] * frames, axis=0) + jnp.sum(
        weight[:, None] * later, axis=0
    )
    feature_sums, pair_count = lax.psum((local_sums, jnp.sum(weight)), "tm")
    center = feature_sums / (2.0 * pair_count)
    early = (weight[:, None] * (frames - center[None, :])).astype(jnp.bfloat16)
    late = (weight[:, None] * (later - center[None, :])).astype(jnp.bfloat16)
    per_column = lax.axis_size("tile") // lax.axis_size("tm")
    first_block = lax.axis_index("tm") * per_column
    rows_early, rows_late = (
        lax.all_gather(early, "tm", axis=0, tiled=True),
        lax.all_gather(late, "tm", axis=0, tiled=True),
    )
    early_parts = []
    late_parts = []
    for member in range(per_column):
        got_early, got_late = (
            broadcast(rows_early, "tile", first_block + member),
            broadcast(rows_late, "tile", first_block + member),
        )
        early_parts.append(got_early)
        late_parts.append(got_late)
    cols_early = jnp.concatenate(early_parts, axis=1)
    cols_late = jnp.concatenate(late_parts, axis=1)
    stacked = jnp.concatenate([rows_early, rows_late], axis=0)
    paired = jnp.concatenate([cols_early, cols_late], axis=0)
    swapped = jnp.concatenate([cols_late, cols_early], axis=0)
    contract = (((0,), (0,)), ((), ()))
    instant_cov = lax.dot_general(stacked, paired, contract, preferred_element_type=jnp.float32) / (
        2.0 * pair_count
    )
    lagged_cov = lax.dot_general(stacked, swapped, contract, preferred_element_type=jnp.float32) / (
        2.0 * pair_count
    )
    return (instant_cov, lagged_cov)


def solution(mesh):
    return jax.shard_map(
        body,
        mesh=mesh,
        in_specs=(P(("groups", "tm"), "tile"), P(("groups", "tm"))),
        out_specs=(P(("groups", "tile"), "tm"), P(("groups", "tile"), "tm")),
        check_vma=False,
    )
```

profile of v0, /device:TPU:3, one launch (start us, length us, event | category | flops | bytes accessed | tf_op | source)
XLA Modules:
  0.0 422.0 jit_solution(8438196369455083313)
XLA Ops:
  7.2 0.0 copy-start
  7.2 0.0 all-gather.3.cloned.1.call-start
  7.2 2.3 slice.14
  9.5 1.3 collective-permute-start.1
  10.8 0.7 slice.12
  11.5 1.3 collective-permute-start
  12.7 18.6 %collective-permute-done = s32[100]{0:T(128)S(1)} collective-permute-done((s32[100]{0:T(128)S(1)}, s32[100]{0:T(128)S(1)}, u32[]{:S(2)}, u32[]{:S(2)}) %collective-permute-start) | collective-permute-done | bytes 432 | tf_op jit(solution)/shard_map/ppermute | solution.py:12
  31.4 0.7 pad_add_fusion
  32.1 1.4 fusion.14
  33.4 0.0 collective-permute-done.1
  33.4 2.5 multiply_reduce_fusion
  36.0 9.0 %all-reduce = (f32[]{:T(128)}, f32[2048]{0:T(1024)S(1)}) all-reduce(f32[]{:T(128)} %get-tuple-element.8, f32[2048]{0:T(1024)S(1)} %add.27), channel_id=1, replica_groups=mesh['groups'=2,'tile'=4,'tm'=4] {'tm'}, use_global_device_ids=true, to_apply=%region_4.0 | all-reduce | flops 2049 | bytes 16392 | tf_op jit(solution)/shard_map/psum | solution.py:31
  45.7 0.0 copy-done
  45.7 2.0 multiply_convert_fusion
  47.7 0.0 all-gather.3.cloned.1.call-update
  47.8 0.0 all-gather.5.cloned.1.call-start
  47.8 0.7 all-gather.5.cloned.1.call-update
  48.5 0.0 all-reduce.4.cloned.1.call-start
  48.6 81.3 %all-gather.3.cloned.1.call-done = bf16[1024,2048]{1,0:T(8,128)(2,1)} async-done(((bf16[256,2048]{1,0:T(8,128)(2,1)}), bf16[1024,2048]{1,0:T(8,128)(2,1)}) %all-gather.3.cloned.1.call-update) | async-done | bytes 4194320 | tf_op jit(solution)/shard_map/all_gather | solution.py:38
  129.8 7.8 %broadcast_select_fusion.1 = (bf16[1024,2048]{1,0:T(8,128)(2,1)}, bf16[2048,2048]{1,0:T(8,128)(2,1)}) fusion(bf16[1024,2048]{1,0:T(8,128)(2,1)} %all-gather.3.cloned.1.call-done, pred[]{:T(512)S(6)} %eq.8), kind=kLoop, calls=%fused_computation.11 | loop fusion | flops 2097151 | bytes 12582913 | tf_op jit(solution)/shard_map/jit(_where)/select_n | solution.py:17
  137.6 73.1 %all-gather.5.cloned.1.call-done = bf16[1024,2048]{1,0:T(8,128)(2,1)} async-done(((bf16[256,2048]{1,0:T(8,128)(2,1)}), bf16[1024,2048]{1,0:T(8,128)(2,1)}) %all-gather.5.cloned.1.call-update) | async-done | bytes 4194320 | tf_op jit(solution)/shard_map/all_gather | solution.py:39
  210.7 7.7 %broadcast_select_fusion = (bf16[1024,2048]{1,0:T(8,128)(2,1)}, bf16[2048,2048]{1,0:T(8,128)(2,1)}) fusion(bf16[1024,2048]{1,0:T(8,128)(2,1)} %all-gather.5.cloned.1.call-done, pred[]{:T(512)S(6)} %eq.8, bf16[2048,2048]{1,0:T(8,128)(2,1)} %get-tuple-element.11), kind=kLoop, calls=%fused_computation.10 | loop fusion | flops 2097152 | bytes 12582913 | tf_op jit(solution)/shard_map/jit(_where)/select_n | solution.py:17
  218.5 0.0 all-reduce.4.cloned.1.call-update
  218.5 151.1 %all-reduce.4.cloned.1.call-done = (bf16[1024,2048]{1,0:T(8,128)(2,1)}, bf16[1024,2048]{1,0:T(8,128)(2,1)}) async-done(((bf16[1024,2048]{1,0:T(8,128)(2,1)}, bf16[1024,2048]{1,0:T(8,128)(2,1)}), (bf16[1024,2048]{1,0:T(8,128)(2,1)}, bf16[1024,2048]{1,0:T(8,128)(2,1)})) %all-reduce.4.cloned.1.call-update) | async-done | bytes 8388624 | tf_op jit(solution)/shard_map/psum | solution.py:17
  369.6 0.0 copy-start.1
  369.6 0.0 copy-start.2
  369.6 0.0 copy-start.3
  369.6 24.5 %broadcast_divide_fusion = f32[2048,2048]{1,0:T(8,128)} fusion(f32[]{:T(128)S(6)} %mul.18, bf16[2048,2048]{1,0:T(8,128)(2,1)} %get-tuple-element.13, bf16[1024,2048]{1,0:T(8,128)(2,1)} %get-tuple-element.7, bf16[1024,2048]{1,0:T(8,128)(2,1)} %get-tuple-element.6), kind=kOutput, calls=%fused_computation.8 | convolution fusion | flops 17200840704 | bytes 33554436 | tf_op jit(solution)/shard_map/dot_general | solution.py:59
  394.1 0.0 copy-done.1
  394.1 0.0 copy-done.2
  394.1 0.0 copy-done.3
  394.2 21.3 %broadcast_divide_fusion.1 = f32[2048,2048]{1,0:T(8,128)} fusion(f32[]{:T(128)S(6)} %mul.18, bf16[2048,2048]{1,0:T(8,128)(2,1)S(1)} %copy-done.1, bf16[1024,2048]{1,0:T(8,128)(2,1)S(1)} %copy-done.2, bf16[1024,2048]{1,0:T(8,128)(2,1)S(1)} %copy-done.3), kind=kOutput, calls=%fused_computation.9 | convolution fusion | flops 17200840704 | bytes 33554436 | tf_op jit(solution)/shard_map/dot_general | solution.py:56
  (2 shorter events, 0.0 us)
Async XLA Ops:
  7.2 38.5 %copy-start = (f32[256,2048]{1,0:T(8,128)S(1)}, f32[256,2048]{1,0:T(8,128)}, u32[]{:S(2)}) copy-start(f32[256,2048]{1,0:T(8,128)} %param.2) | copy-start | bytes 6291460
  7.2 122.7 %all-gather.3.cloned.1.call-start = ((), (), s32[]{:S(2)}) async-start(), calls=%async_computation | async-start | bytes 5242880 | tf_op jit(solution)/shard_map/all_gather | solution.py:38
  9.5 23.9 %collective-permute-start.1 = (f32[100,2048]{1,0:T(8,128)}, f32[100,2048]{1,0:T(8,128)S(1)}, u32[]{:S(2)}, u32[]{:S(2)}) collective-permute-start(f32[100,2048]{1,0:T(8,128)} %slice.14), channel_id=1, source_target_pairs={{1,0},{2,1},{3,2},{5,4},{6,5},{7,6},{9,8},{10,9},{11,10},{13,12},{... | collective-permute-start | bytes 2457608 | tf_op jit(solution)/shard_map/ppermute | solution.py:12
  11.5 19.9 %collective-permute-start = (s32[100]{0:T(128)S(1)}, s32[100]{0:T(128)S(1)}, u32[]{:S(2)}, u32[]{:S(2)}) collective-permute-start(s32[100]{0:T(128)S(1)} %slice.12), channel_id=1, source_target_pairs={{1,0},{2,1},{3,2},{5,4},{6,5},{7,6},{9,8},{10,9},{11,10},{13,12},{... | collective-permute-start | bytes 1208 | tf_op jit(solution)/shard_map/ppermute | solution.py:12
  47.8 163.0 %all-gather.5.cloned.1.call-start = ((), (), s32[]{:S(2)}) async-start(), calls=%async_computation.1 | async-start | bytes 5242880 | tf_op jit(solution)/shard_map/all_gather | solution.py:39
  48.5 321.1 %all-reduce.4.cloned.1.call-start = ((), (), s32[]{:S(2)}) async-start(), calls=%async_computation.2 | async-start | bytes 16777216 | tf_op jit(solution)/shard_map/psum | solution.py:17
  369.6 24.5 %copy-start.1 = (bf16[2048,2048]{1,0:T(8,128)(2,1)S(1)}, bf16[2048,2048]{1,0:T(8,128)(2,1)}, u32[]{:S(2)}) copy-start(bf16[2048,2048]{1,0:T(8,128)(2,1)} %get-tuple-element.13) | copy-start | bytes 25165828
  369.6 24.5 %copy-start.2 = (bf16[1024,2048]{1,0:T(8,128)(2,1)S(1)}, bf16[1024,2048]{1,0:T(8,128)(2,1)}, u32[]{:S(2)}) copy-start(bf16[1024,2048]{1,0:T(8,128)(2,1)} %get-tuple-element.6) | copy-start | bytes 12582916
  369.6 24.5 %copy-start.3 = (bf16[1024,2048]{1,0:T(8,128)(2,1)S(1)}, bf16[1024,2048]{1,0:T(8,128)(2,1)}, u32[]{:S(2)}) copy-start(bf16[1024,2048]{1,0:T(8,128)(2,1)} %get-tuple-element.7) | copy-start | bytes 12582916
Sparse Core Ops, SparseCore 0:
  47.9 81.9 all-gather.2
  131.4 79.2 all-gather.4
  218.6 150.9 all-reduce.3
where the time goes:
time: 425 us; the launch traced here: 422 us
  waiting for transfers between devices  325 us (76%)
  matrix products  45.8 us (11%)
  other arithmetic  22.1 us (5%)
  between operations  14.5 us (3%)
  blocking collectives  9 us (2%)
    psum x1, waiting for transfers between devices, broadcast(): return lax.psum(jnp.where(mine, x, jnp.zeros_like(x)), axis)  151 us
    all_gather x1, waiting for transfers between devices, body(): lax.all_gather(early, 'tm', axis=0, tiled=True)  81.3 us
    all_gather x1, waiting for transfers between devices, body(): lax.all_gather(late, 'tm', axis=0, tiled=True)  73.1 us
    dot_general x1, matrix products, body(): lax.dot_general(stacked, swapped, contract, preferred_element_type=jnp.fl...  24.5 us
    dot_general x1, matrix products, body(): lax.dot_general(stacked, paired, contract, preferred_element_type=jnp.flo...  21.3 us
    ppermute x2, waiting for transfers between devices, from_behind(): lax.ppermute(value, axis, [(source, source + steps) for source in range(i...  18.6 us
    select_n x2, other arithmetic, broadcast(): return lax.psum(jnp.where(mine, x, jnp.zeros_like(x)), axis)  15.5 us
    psum x1, blocking collectives, body(): feature_sums, pair_count = lax.psum((local_sums, jnp.sum(weight)), 'tm')  9 us
  transfers between devices with their start and end apart: 5, of which 4 were waited for; matrix products, arithmetic and copies ran while one was open for 2% of the time, Pallas kernels for 0%

commit v1 on v0

v1 whole, which is shorter than its diff:
```python
import functools

import jax
import jax.numpy as jnp
from jax import lax
from jax.experimental import pallas as pl
from jax.experimental.pallas import tpu as pltpu
from jax.sharding import PartitionSpec as P

LAG = 100
LANES = 128
PIECES = 2
MESH = pl.DeviceIdType.MESH


def aligned(value, step):
    return pl.multiple_of(value, step)


def gather_kernel(
    n, tiles, pc,
    frames_ref, seg_ref,
    sum_t_ref, dif_t_ref, cols_ref, weight_ref, scale_ref,
    rows, seg_all, v_all, sums_all,
    seg_send, seg_recv, tot_send, tot_recv,
    up_send, down_send, row_recv, xup_send, xdown_send, sib_send, col_recv, own_sem,
):
    slab_rows, width = frames_ref.shape
    total = n * slab_rows
    piece = slab_rows // PIECES
    z = lax.axis_index("tm")
    t = lax.axis_index("tile")
    x, core = t // 2, t % 2
    sibling = x * 2 + (1 - core)
    last_x = tiles // 2 - 1
    right, left = (t + 2) % tiles, (t + tiles - 2) % tiles

    barrier = pltpu.get_barrier_semaphore()
    for step in range(1, n):
        pl.semaphore_signal(barrier, inc=1, device_id={"tm": (z + step) % n}, device_id_type=MESH)
    for other in (sibling, right, left):
        pl.semaphore_signal(barrier, inc=1, device_id={"tile": other}, device_id_type=MESH)
    pl.semaphore_wait(barrier, n - 1 + 3)

    def to_all(buffer, send, recv):
        return [
            pltpu.make_async_remote_copy(
                src_ref=buffer.at[z], dst_ref=buffer.at[z],
                send_sem=send.at[step], recv_sem=recv.at[step],
                device_id={"tm": (z + step) % n}, device_id_type=MESH,
            )
            for step in range(1, n)
        ]

    seg_all[z] = seg_ref[...]
    copies = to_all(seg_all, seg_send, seg_recv)
    for copy in copies:
        copy.start()
    rows[total:, :] = jnp.zeros((LANES, width), jnp.bfloat16)
    for copy in copies:
        copy.wait()
    seg = jnp.concatenate([seg_all[slab] for slab in range(n)], axis=1)
    places = lax.broadcasted_iota(jnp.int32, seg.shape, 1)
    same = (seg == pltpu.roll(seg, total - LAG, 1)) & (places + LAG < total)
    weight = jnp.where(same, 1.0, 0.0).astype(jnp.float32)
    pairs = jnp.sum(weight, axis=1, keepdims=True)
    uses = weight + pltpu.roll(weight, LAG, 1)
    for slab in range(n):
        v_all[slab] = uses[:, slab * slab_rows : (slab + 1) * slab_rows]
    scale_ref[...] = jnp.broadcast_to(0.25 / pairs, scale_ref.shape)

    parts = width // LANES
    local = jnp.dot(
        v_all[z], frames_ref[...],
        precision=lax.Precision.HIGHEST, preferred_element_type=jnp.float32,
    )
    for part in range(parts):
        sums_all[z, part : part + 1, :] = local[0:1, part * LANES : (part + 1) * LANES]
    copies = to_all(sums_all, tot_send, tot_recv)
    for copy in copies:
        copy.start()
    for slab in range(n):
        column = weight[0:1, slab * slab_rows : (slab + 1) * slab_rows]
        weight_ref[slab * slab_rows : (slab + 1) * slab_rows, :] = jnp.broadcast_to(
            column, (LANES, slab_rows)
        ).T
    for copy in copies:
        copy.wait()
    sums = sums_all[0]
    for slab in range(1, n):
        sums = sums + sums_all[slab]
    center = sums / (2.0 * pairs[0:1, 0:1])

    def span(slab, k):
        return pl.ds(aligned(slab * slab_rows + k * piece, piece), piece)

    def row_copy(slab, k, up):
        here = rows.at[span(slab, k)]
        return pltpu.make_async_remote_copy(
            src_ref=here, dst_ref=here,
            send_sem=(up_send if up else down_send).at[slab, k],
            recv_sem=row_recv.at[slab, k],
            device_id={"tm": jnp.minimum(z + 1, n - 1) if up else jnp.maximum(z - 1, 0)},
            device_id_type=MESH,
        )

    def col_copy(m, slab, k, where, source):
        there = cols_ref.at[m, span(slab, k)]
        send, dev = {
            "sib": (sib_send, sibling),
            "up": (xup_send, right),
            "down": (xdown_send, left),
        }[where]
        return pltpu.make_async_remote_copy(
            src_ref=rows.at[span(slab, k)] if source else there, dst_ref=there,
            send_sem=send.at[m, slab, k], recv_sem=col_recv.at[m, slab, k],
            device_id={"tile": dev}, device_id_type=MESH,
        )

    def own_copy(m, slab, k):
        return pltpu.make_async_copy(
            rows.at[span(slab, k)], cols_ref.at[m, span(slab, k)], own_sem.at[m, slab, k]
        )

    def roles(m):
        source = z * pc + m
        is_source = t == source
        relay = (core == source % 2) & (t != source)
        goes_up = (x < last_x) & (x >= source // 2)
        goes_down = (x > 0) & (x <= source // 2)
        return is_source, relay, goes_up, goes_down

    def each_column(slab, k, from_rows, act):
        for m in range(pc):
            is_source, relay, goes_up, goes_down = roles(m)
            if from_rows:
                @pl.when(is_source)
                def _():
                    own = own_copy(m, slab, k)
                    own.start() if act is start else own.wait()
                    act(col_copy(m, slab, k, "sib", True))

                @pl.when(is_source & goes_up)
                def _():
                    act(col_copy(m, slab, k, "up", True))

                @pl.when(is_source & goes_down)
                def _():
                    act(col_copy(m, slab, k, "down", True))
            else:
                @pl.when(relay & goes_up)
                def _():
                    act(col_copy(m, slab, k, "up", False))

                @pl.when(relay & goes_down)
                def _():
                    act(col_copy(m, slab, k, "down", False))

                @pl.when(relay)
                def _():
                    act(col_copy(m, slab, k, "sib", False))

    start = lambda copy: copy.start()

    sent = lambda copy: copy.wait_send()

    def column_arrives(slab, k):
        for m in range(pc):
            is_source = roles(m)[0]

            @pl.when(jnp.logical_not(is_source))
            def _():
                col_copy(m, slab, k, "sib", False).wait_recv()

        each_column(slab, k, False, start)

    def prepare(slab):
        base = aligned(slab * slab_rows, slab_rows)
        w = weight_ref[pl.ds(base, slab_rows), :]

        @pl.loop(0, parts)
        def _(part):
            at = aligned(part * LANES, LANES)
            c = rows[pl.ds(base, slab_rows + LANES), pl.ds(at, LANES)].astype(jnp.float32)
            now = c[:slab_rows]
            lagged = pltpu.roll(c, slab_rows + LANES - LAG, 0)[:slab_rows]
            sum_t_ref[pl.ds(at, LANES), pl.ds(base, slab_rows)] = (
                (w * (now + lagged)).T.astype(jnp.bfloat16)
            )
            dif_t_ref[pl.ds(at, LANES), pl.ds(base, slab_rows)] = (
                (w * (now - lagged)).T.astype(jnp.bfloat16)
            )

    for k in range(PIECES):
        for part in range(parts):
            at = slice(part * LANES, (part + 1) * LANES)
            rows[span(z, k), at] = (
                frames_ref[k * piece : (k + 1) * piece, at] - center[part : part + 1, :]
            ).astype(jnp.bfloat16)

        @pl.when(z < n - 1)
        def _():
            row_copy(z, k, True).start()

        @pl.when(z > 0)
        def _():
            row_copy(z, k, False).start()

        each_column(z, k, True, start)

    def row_arrives(d, k):
        below, above = z - d, z + d

        @pl.when(below >= 0)
        def _():
            row_copy(below, k, True).wait_recv()

            @pl.when(z < n - 1)
            def _():
                row_copy(below, k, True).start()

            each_column(below, k, True, start)

        @pl.when(above < n)
        def _():
            row_copy(above, k, False).wait_recv()

            @pl.when(z > 0)
            def _():
                row_copy(above, k, False).start()

            each_column(above, k, True, start)

    def columns_arrive(d, k):
        if d == 0:
            column_arrives(z, k)
            return

        @pl.when(z - d >= 0)
        def _():
            column_arrives(z - d, k)

        @pl.when(z + d < n)
        def _():
            column_arrives(z + d, k)

    steps = [(d, k) for d in range(n) for k in range(PIECES)]
    behind = 0
    for index, (d, k) in enumerate(steps):
        if d > 0:
            row_arrives(d, k)
            columns_arrive(*steps[behind])
            behind += 1
        if k == PIECES - 1:
            if d > 0:
                @pl.when(z - d >= 0)
                def _():
                    prepare(z - d)

                @pl.when(z + d < n)
                def _():
                    prepare(z + d - 1)

            @pl.when(z + d == n - 1)
            def _():
                prepare(n - 1)

    for entry in steps[behind:]:
        columns_arrive(*entry)

    for slab in range(n):
        for k in range(PIECES):
            @pl.when((z < n - 1) & (slab <= z))
            def _():
                row_copy(slab, k, True).wait_send()

            @pl.when((z > 0) & (slab >= z))
            def _():
                row_copy(slab, k, False).wait_send()

            each_column(slab, k, True, sent)
            each_column(slab, k, False, sent)


def product_kernel(sum_t_ref, dif_t_ref, cols_ref, weight_ref, scale_ref, inst_ref, lag_ref, plus, minus):
    total, wide = plus.shape
    for part in range(wide // LANES):
        at = slice(part * LANES, (part + 1) * LANES)
        c = cols_ref[0, :, at].astype(jnp.float32)
        lagged = pltpu.roll(c, total - LAG, 0)
        w = weight_ref[...]
        plus[:, at] = (w * (c + lagged)).astype(jnp.bfloat16)
        minus[:, at] = (w * (c - lagged)).astype(jnp.bfloat16)
    height = sum_t_ref.shape[0]
    block = min(512, height)
    scale = scale_ref[0:1, 0:1]
    for index in range(height // block):
        at = slice(index * block, (index + 1) * block)
        a = jnp.dot(sum_t_ref[at, :], plus[...], preferred_element_type=jnp.float32)
        b = jnp.dot(dif_t_ref[at, :], minus[...], preferred_element_type=jnp.float32)
        inst_ref[at, :] = (a + b) * scale
        lag_ref[at, :] = (a - b) * scale


def body(frames, segment_ids):
    n, tiles = lax.axis_size("tm"), lax.axis_size("tile")
    pc = tiles // n
    slab_rows, width = frames.shape
    total = n * slab_rows
    sum_rows = -(-(width // LANES) // 8) * 8
    seg = jnp.broadcast_to(segment_ids[None, :], (8, slab_rows))
    vmem = pl.BlockSpec(memory_space=pltpu.VMEM)
    dma = pltpu.SemaphoreType.DMA
    sum_t, dif_t, cols, weight, scale = pl.pallas_call(
        functools.partial(gather_kernel, n, tiles, pc),
        out_shape=(
            jax.ShapeDtypeStruct((width, total), jnp.bfloat16),
            jax.ShapeDtypeStruct((width, total), jnp.bfloat16),
            jax.ShapeDtypeStruct((pc, total, width), jnp.bfloat16),
            jax.ShapeDtypeStruct((total, LANES), jnp.float32),
            jax.ShapeDtypeStruct((8, LANES), jnp.float32),
        ),
        in_specs=[vmem, vmem],
        out_specs=(vmem, vmem, pl.BlockSpec(memory_space=pl.ANY), vmem, vmem),
        scratch_shapes=[
            pltpu.VMEM((total + LANES, width), jnp.bfloat16),
            pltpu.VMEM((n, 8, slab_rows), jnp.int32),
            pltpu.VMEM((n, 8, slab_rows), jnp.float32),
            pltpu.VMEM((n, sum_rows, LANES), jnp.float32),
            dma((n,)), dma((n,)), dma((n,)), dma((n,)),
            dma((n, PIECES)), dma((n, PIECES)), dma((n, PIECES)),
            dma((pc, n, PIECES)), dma((pc, n, PIECES)), dma((pc, n, PIECES)),
            dma((pc, n, PIECES)), dma((pc, n, PIECES)),
        ],
        compiler_params=pltpu.CompilerParams(
            collective_id=0, has_side_effects=True, vmem_limit_bytes=44 * 1024 * 1024
        ),
    )(frames, seg)

    wide = min(256, width)
    per_tile = width // wide
    out = jax.ShapeDtypeStruct((width, pc * width), jnp.float32)
    whole = pl.BlockSpec((width, total), lambda j: (0, 0))
    tile = pl.BlockSpec((width, wide), lambda j: (0, j))
    return pl.pallas_call(
        product_kernel,
        grid=(pc * per_tile,),
        out_shape=(out, out),
        in_specs=[
            whole, whole,
            pl.BlockSpec((1, total, wide), lambda j: (j // per_tile, 0, j % per_tile)),
            pl.BlockSpec((total, LANES), lambda j: (0, 0)),
            pl.BlockSpec((8, LANES), lambda j: (0, 0)),
        ],
        out_specs=(tile, tile),
        scratch_shapes=[pltpu.VMEM((total, wide), jnp.bfloat16)] * 2,
        compiler_params=pltpu.CompilerParams(vmem_limit_bytes=44 * 1024 * 1024),
        cost_estimate=pl.CostEstimate(
            flops=4 * total * width * width * pc,
            bytes_accessed=8 * width * width * pc + 6 * total * width,
            transcendentals=0,
        ),
    )(sum_t, dif_t, cols, weight, scale)


def solution(mesh):
    return jax.shard_map(
        body,
        mesh=mesh,
        in_specs=(P(("groups", "tm"), "tile"), P(("groups", "tm"))),
        out_specs=(P(("groups", "tile"), "tm"), P(("groups", "tile"), "tm")),
        check_vma=False,
    )
```

time: 425 us -> 121 us (0.28)
  waiting for transfers between devices: 325 us -> 0 us
  Pallas kernels: 0 us -> 115 us
  matrix products: 45.8 us -> 0 us
  other arithmetic: 22.1 us -> 0 us
  between operations: 14.5 us -> 0.65 us
  blocking collectives: 9 us -> 0 us
    all_gather x2 -> x0, waiting for transfers between devices: 154 us -> none  [the longest x1 81.3 us: body(): lax.all_gather(early, 'tm', axis=0, tiled=True)]
    psum x1 -> x0, waiting for transfers between devices: 151 us -> none  [broadcast(): return lax.psum(jnp.where(mine, x, jnp.zeros_like(x)), axis)]
    pallas_call x0 -> x2, Pallas kernels: none -> 115 us  [the longest x1 91.8 us: body(): pl.pallas_call(functools.partial(gather_kernel, n, tiles, pc), out_shape=...]
    dot_general x2 -> x0, matrix products: 45.8 us -> none  [the longest x1 24.5 us: body(): lax.dot_general(stacked, swapped, contract, preferred_element_type=jnp.fl...]
    ppermute x2 -> x0, waiting for transfers between devices: 18.6 us -> none  [from_behind(): lax.ppermute(value, axis, [(source, source + steps) for source in range(i...]
    select_n x2 -> x0, other arithmetic: 15.5 us -> none  [broadcast(): return lax.psum(jnp.where(mine, x, jnp.zeros_like(x)), axis)]
    psum x1 -> x0, blocking collectives: 9 us -> none  [body(): feature_sums, pair_count = lax.psum((local_sums, jnp.sum(weight)), 'tm')]
  transfers between devices with their start and end apart: 5 -> 0, of which waited for: 4 -> 0; matrix products, arithmetic and copies ran while one was open for 2% -> 0% of each run, Pallas kernels for 0% -> 0%
where the time goes in v1:
time: 121 us; the launch traced here: 120 us
  Pallas kernels  115 us (95%)
  local copies, waits for them, and re-layouts  4.45 us (4%)
    pallas_call x1, Pallas kernels, body(): pl.pallas_call(functools.partial(gather_kernel, n, tiles, pc), out_shape=...  91.8 us
    pallas_call x1, Pallas kernels, body(): pl.pallas_call(product_kernel, grid=(pc * per_tile,), out_shape=(out, out...  23.4 us
    unnamed x4, local copies, waits for them, and re-layouts  3.77 us

profile of v1, /device:TPU:3, one launch (start us, length us, event | category | flops | bytes accessed | tf_op | source)
XLA Modules:
  0.0 120.3 jit_solution(18027848816824017413)
XLA Ops:
  0.6 0.7 broadcast_in_dim.2.seg_ref
  1.3 0.0 copy-start
  1.3 1.6 %copy-done = f32[256,2048]{1,0:T(8,128)S(1)} copy-done((f32[256,2048]{1,0:T(8,128)S(1)}, f32[256,2048]{1,0:T(8,128)}, u32[]{:S(2)}) %copy-start) | copy-done | bytes 2097176
  2.9 91.8 %shard_map.41 = (bf16[2048,1024]{1,0:T(8,128)(2,1)S(1)}, bf16[2048,1024]{1,0:T(8,128)(2,1)}, bf16[1,1024,2048]{2,1,0:T(8,128)(2,1)}, f32[1024,128]{1,0:T(8,128)S(1)}, f32[8,128]{1,0:T(8,128)S(1)}) custom-call(f32[256,2048]{1,0:T(8,128)S(1)} %copy-done, s32[8,256]{1,0:T(8,128)S(1)} %broadcast_in_dim.2.seg_ref), custom_call_target="tpu_custom_call" | custom-call | tf_op jit(solution)/shard_map/pallas_call | solution.py:314
  94.7 0.0 copy-start.1
  94.7 2.2 %copy-done.1 = bf16[2048,1024]{1,0:T(8,128)(2,1)S(1)} copy-done((bf16[2048,1024]{1,0:T(8,128)(2,1)S(1)}, bf16[2048,1024]{1,0:T(8,128)(2,1)}, u32[]{:S(2)}) %copy-start.1) | copy-done | bytes 4194328
  96.9 23.4 %shard_map.42 = (f32[2048,2048]{1,0:T(8,128)}, f32[2048,2048]{1,0:T(8,128)}) custom-call(bf16[2048,1024]{1,0:T(8,128)(2,1)S(1)} %get-tuple-element.7.sum_t_ref, bf16[2048,1024]{1,0:T(8,128)(2,1)S(1)} %copy-done.1, bf16[1,1024,2048]{2,1,0:T(8,128)(2,1)} %get-tuple-element.9.cols_ref, f32[1024,128]{1,0:T(8,128)S(1)} %get-tuple-element.10.weight_ref, ...), custom_call_target="tpu_custom_call" | custom-call | flops 17179869184 | bytes 46137344 | tf_op jit(solution)/shard_map/pallas_call | solution.py:345
Async XLA Ops:
  1.3 1.6 %copy-start = (f32[256,2048]{1,0:T(8,128)S(1)}, f32[256,2048]{1,0:T(8,128)}, u32[]{:S(2)}) copy-start(f32[256,2048]{1,0:T(8,128)} %frames_ref.1) | copy-start | bytes 6291460
  94.7 2.2 %copy-start.1 = (bf16[2048,1024]{1,0:T(8,128)(2,1)S(1)}, bf16[2048,1024]{1,0:T(8,128)(2,1)}, u32[]{:S(2)}) copy-start(bf16[2048,1024]{1,0:T(8,128)(2,1)} %get-tuple-element.8.dif_t_ref) | copy-start | bytes 12582916

commit v2 on v1

--- a/solution.py
+++ b/solution.py
@@ -9,7 +9,7 @@
 
 LAG = 100
 LANES = 128
-PIECES = 2
+PIECES = 4
 MESH = pl.DeviceIdType.MESH
 
 
@@ -245,22 +245,24 @@
             column_arrives(z + d, k)
 
     steps = [(d, k) for d in range(n) for k in range(PIECES)]
-    behind = 0
+    behind, ahead = 0, -(-LANES // piece) - 1
     for index, (d, k) in enumerate(steps):
         if d > 0:
             row_arrives(d, k)
-            columns_arrive(*steps[behind])
-            behind += 1
+            while behind < index:
+                columns_arrive(*steps[behind])
+                behind += 1
+        if d > 0 and k == ahead:
+            @pl.when(z + d < n)
+            def _():
+                prepare(z + d - 1)
+
         if k == PIECES - 1:
             if d > 0:
                 @pl.when(z - d >= 0)
                 def _():
                     prepare(z - d)
 
-                @pl.when(z + d < n)
-                def _():
-                    prepare(z + d - 1)
-
             @pl.when(z + d == n - 1)
             def _():
                 prepare(n - 1)
@@ -282,24 +284,51 @@
             each_column(slab, k, False, sent)
 
 
-def product_kernel(sum_t_ref, dif_t_ref, cols_ref, weight_ref, scale_ref, inst_ref, lag_ref, plus, minus):
-    total, wide = plus.shape
-    for part in range(wide // LANES):
+def product_kernel(
+    sum_t_ref, dif_t_ref, first_ref, next_ref, weight_ref, scale_ref, inst_ref, lag_ref,
+    plus_0, minus_0, plus_1, minus_1,
+):
+    total, wide = plus_0.shape
+    height = sum_t_ref.shape[0]
+    block = min(512, height)
+    blocks, parts = height // block, wide // LANES
+    scale = scale_ref[0:1, 0:1]
+    j = pl.program_id(0)
+
+    def prepare(part, block_ref, plus, minus):
         at = slice(part * LANES, (part + 1) * LANES)
-        c = cols_ref[0, :, at].astype(jnp.float32)
+        c = block_ref[0, :, at].astype(jnp.float32)
         lagged = pltpu.roll(c, total - LAG, 0)
         w = weight_ref[...]
         plus[:, at] = (w * (c + lagged)).astype(jnp.bfloat16)
         minus[:, at] = (w * (c - lagged)).astype(jnp.bfloat16)
-    height = sum_t_ref.shape[0]
-    block = min(512, height)
-    scale = scale_ref[0:1, 0:1]
-    for index in range(height // block):
-        at = slice(index * block, (index + 1) * block)
-        a = jnp.dot(sum_t_ref[at, :], plus[...], preferred_element_type=jnp.float32)
-        b = jnp.dot(dif_t_ref[at, :], minus[...], preferred_element_type=jnp.float32)
-        inst_ref[at, :] = (a + b) * scale
-        lag_ref[at, :] = (a - b) * scale
+
+    def multiply(now, later):
+        ready = 0
+        for index in range(blocks):
+            at = slice(index * block, (index + 1) * block)
+            a = jnp.dot(sum_t_ref[at, :], now[0][...], preferred_element_type=jnp.float32)
+            b = jnp.dot(dif_t_ref[at, :], now[1][...], preferred_element_type=jnp.float32)
+            inst_ref[at, :] = (a + b) * scale
+            lag_ref[at, :] = (a - b) * scale
+            while ready * blocks < (index + 1) * parts:
+                prepare(ready, next_ref, *later)
+                ready += 1
+
+    even, odd = (plus_0, minus_0), (plus_1, minus_1)
+
+    @pl.when(j == 0)
+    def _():
+        for part in range(parts):
+            prepare(part, first_ref, *even)
+
+    @pl.when(j % 2 == 0)
+    def _():
+        multiply(even, odd)
+
+    @pl.when(j % 2 == 1)
+    def _():
+        multiply(odd, even)
 
 
 def body(frames, segment_ids):
@@ -333,7 +362,7 @@
             dma((pc, n, PIECES)), dma((pc, n, PIECES)),
         ],
         compiler_params=pltpu.CompilerParams(
-            collective_id=0, has_side_effects=True, vmem_limit_bytes=44 * 1024 * 1024
+            collective_id=0, has_side_effects=True, vmem_limit_bytes=28 * 1024 * 1024
         ),
     )(frames, seg)
 
@@ -341,6 +370,12 @@
     per_tile = width // wide
     out = jax.ShapeDtypeStruct((width, pc * width), jnp.float32)
     whole = pl.BlockSpec((width, total), lambda j: (0, 0))
+    last = pc * per_tile - 1
+
+    def next_block(j):
+        following = jnp.minimum(j + 1, last)
+        return following // per_tile, 0, following % per_tile
+
     tile = pl.BlockSpec((width, wide), lambda j: (0, j))
     return pl.pallas_call(
         product_kernel,
@@ -348,19 +383,20 @@
         out_shape=(out, out),
         in_specs=[
             whole, whole,
-            pl.BlockSpec((1, total, wide), lambda j: (j // per_tile, 0, j % per_tile)),
+            pl.BlockSpec((1, total, wide), lambda j: (0, 0, 0)),
+            pl.BlockSpec((1, total, wide), next_block),
             pl.BlockSpec((total, LANES), lambda j: (0, 0)),
             pl.BlockSpec((8, LANES), lambda j: (0, 0)),
         ],
         out_specs=(tile, tile),
-        scratch_shapes=[pltpu.VMEM((total, wide), jnp.bfloat16)] * 2,
-        compiler_params=pltpu.CompilerParams(vmem_limit_bytes=44 * 1024 * 1024),
+        scratch_shapes=[pltpu.VMEM((total, wide), jnp.bfloat16)] * 4,
+        compiler_params=pltpu.CompilerParams(vmem_limit_bytes=36 * 1024 * 1024),
         cost_estimate=pl.CostEstimate(
             flops=4 * total * width * width * pc,
             bytes_accessed=8 * width * width * pc + 6 * total * width,
             transcendentals=0,
         ),
-    )(sum_t, dif_t, cols, weight, scale)
+    )(sum_t, dif_t, cols, cols, weight, scale)
 
 
 def solution(mesh):

time: 121 us -> 117 us (0.967)
  local copies, waits for them, and re-layouts: 4.45 us -> 2.27 us
    pallas_call x1, Pallas kernels: 91.8 us -> 86.7 us  [body(): pl.pallas_call(functools.partial(gather_kernel, n, tiles, pc), out_shape=...]
    pallas_call x1, Pallas kernels: 23.4 us -> 27.6 us  [body(): pl.pallas_call(product_kernel, grid=(pc * per_tile,), out_shape=(out, out...]
    unnamed x4 -> x2, local copies, waits for them, and re-layouts: 3.77 us -> 1.59 us
where the time goes in v2:
time: 117 us
  Pallas kernels  114 us (97%)
  local copies, waits for them, and re-layouts  2.27 us (2%)
    pallas_call x1, Pallas kernels, body(): pl.pallas_call(functools.partial(gather_kernel, n, tiles, pc), out_shape=...  86.7 us
    pallas_call x1, Pallas kernels, body(): pl.pallas_call(product_kernel, grid=(pc * per_tile,), out_shape=(out, out...  27.6 us

profile of v2, /device:TPU:3, one launch (start us, length us, event | category | flops | bytes accessed | tf_op | source)
XLA Modules:
  0.0 117.2 jit_solution(13132490394124077719)
XLA Ops:
  0.6 0.7 broadcast_in_dim.2.seg_ref
  1.3 0.0 copy-start
  1.3 1.6 %copy-done = f32[256,2048]{1,0:T(8,128)S(1)} copy-done((f32[256,2048]{1,0:T(8,128)S(1)}, f32[256,2048]{1,0:T(8,128)}, u32[]{:S(2)}) %copy-start) | copy-done | bytes 2097176
  2.9 86.7 %shard_map.41 = (bf16[2048,1024]{1,0:T(8,128)(2,1)S(1)}, bf16[2048,1024]{1,0:T(8,128)(2,1)S(1)}, bf16[1,1024,2048]{2,1,0:T(8,128)(2,1)S(1)}, f32[1024,128]{1,0:T(8,128)S(1)}, f32[8,128]{1,0:T(8,128)S(1)}) custom-call(f32[256,2048]{1,0:T(8,128)S(1)} %copy-done, s32[8,256]{1,0:T(8,128)S(1)} %broadcast_in_dim.2.seg_ref), custom_call_target="tpu_custom_call" | custom-call | tf_op jit(solution)/shard_map/pallas_call | solution.py:343
  89.7 27.6 %shard_map.42 = (f32[2048,2048]{1,0:T(8,128)}, f32[2048,2048]{1,0:T(8,128)}) custom-call(bf16[2048,1024]{1,0:T(8,128)(2,1)S(1)} %get-tuple-element.7.sum_t_ref, bf16[2048,1024]{1,0:T(8,128)(2,1)S(1)} %get-tuple-element.8.dif_t_ref, bf16[1,1024,2048]{2,1,0:T(8,128)(2,1)S(1)} %get-tuple-element.9.first_ref.next_ref, ...), custom_call_target="tpu_custom_call" | custom-call | flops 17179869184 | bytes 46137344 | tf_op jit(solution)/shard_map/pallas_call | solution.py:380
Async XLA Ops:
  1.3 1.6 %copy-start = (f32[256,2048]{1,0:T(8,128)S(1)}, f32[256,2048]{1,0:T(8,128)}, u32[]{:S(2)}) copy-start(f32[256,2048]{1,0:T(8,128)} %frames_ref.1) | copy-start | bytes 6291460

commit v3 on v1

--- a/solution.py
+++ b/solution.py
@@ -9,7 +9,7 @@
 
 LAG = 100
 LANES = 128
-PIECES = 2
+PIECES = 4
 MESH = pl.DeviceIdType.MESH
 
 
@@ -20,8 +20,8 @@
 def gather_kernel(
     n, tiles, pc,
     frames_ref, seg_ref,
-    sum_t_ref, dif_t_ref, cols_ref, weight_ref, scale_ref,
-    rows, seg_all, v_all, sums_all,
+    sum_t_ref, dif_t_ref, plus_ref, minus_ref, scale_ref,
+    rows, cols_ref, weight_ref, seg_all, v_all, sums_all,
     seg_send, seg_recv, tot_send, tot_recv,
     up_send, down_send, row_recv, xup_send, xdown_send, sib_send, col_recv, own_sem,
 ):
@@ -57,6 +57,8 @@
     for copy in copies:
         copy.start()
     rows[total:, :] = jnp.zeros((LANES, width), jnp.bfloat16)
+    for m in range(pc):
+        cols_ref[m, total:, :] = jnp.zeros((LANES, width), jnp.bfloat16)
     for copy in copies:
         copy.wait()
     seg = jnp.concatenate([seg_all[slab] for slab in range(n)], axis=1)
@@ -136,8 +138,8 @@
             if from_rows:
                 @pl.when(is_source)
                 def _():
-                    own = own_copy(m, slab, k)
-                    own.start() if act is start else own.wait()
+                    if act is start:
+                        own_copy(m, slab, k).start()
                     act(col_copy(m, slab, k, "sib", True))
 
                 @pl.when(is_source & goes_up)
@@ -167,6 +169,10 @@
     def column_arrives(slab, k):
         for m in range(pc):
             is_source = roles(m)[0]
+
+            @pl.when(is_source)
+            def _():
+                own_copy(m, slab, k).wait()
 
             @pl.when(jnp.logical_not(is_source))
             def _():
@@ -191,6 +197,19 @@
                 (w * (now - lagged)).T.astype(jnp.bfloat16)
             )
 
+    def prepare_columns(slab):
+        base = aligned(slab * slab_rows, slab_rows)
+        w = weight_ref[pl.ds(base, slab_rows), :]
+        for m in range(pc):
+            @pl.loop(0, parts)
+            def _(part):
+                at = pl.ds(aligned(part * LANES, LANES), LANES)
+                c = cols_ref[m, pl.ds(base, slab_rows + LANES), at].astype(jnp.float32)
+                now = c[:slab_rows]
+                lagged = pltpu.roll(c, slab_rows + LANES - LAG, 0)[:slab_rows]
+                plus_ref[m, pl.ds(base, slab_rows), at] = (w * (now + lagged)).astype(jnp.bfloat16)
+                minus_ref[m, pl.ds(base, slab_rows), at] = (w * (now - lagged)).astype(jnp.bfloat16)
+
     for k in range(PIECES):
         for part in range(parts):
             at = slice(part * LANES, (part + 1) * LANES)
@@ -231,39 +250,45 @@
 
             each_column(above, k, True, start)
 
+    def ready(d, k, form):
+        if d > 0 and k == ahead:
+            @pl.when(z + d < n)
+            def _():
+                form(z + d - 1)
+
+        if k == PIECES - 1:
+            if d > 0:
+                @pl.when(z - d >= 0)
+                def _():
+                    form(z - d)
+
+            @pl.when(z + d == n - 1)
+            def _():
+                form(n - 1)
+
     def columns_arrive(d, k):
         if d == 0:
             column_arrives(z, k)
-            return
-
-        @pl.when(z - d >= 0)
-        def _():
-            column_arrives(z - d, k)
-
-        @pl.when(z + d < n)
-        def _():
-            column_arrives(z + d, k)
+        else:
+            @pl.when(z - d >= 0)
+            def _():
+                column_arrives(z - d, k)
+
+            @pl.when(z + d < n)
+            def _():
+                column_arrives(z + d, k)
+
+        ready(d, k, prepare_columns)
 
     steps = [(d, k) for d in range(n) for k in range(PIECES)]
-    behind = 0
+    behind, ahead = 0, -(-LANES // piece) - 1
     for index, (d, k) in enumerate(steps):
         if d > 0:
             row_arrives(d, k)
-            columns_arrive(*steps[behind])
-            behind += 1
-        if k == PIECES - 1:
-            if d > 0:
-                @pl.when(z - d >= 0)
-                def _():
-                    prepare(z - d)
-
-                @pl.when(z + d < n)
-                def _():
-                    prepare(z + d - 1)
-
-            @pl.when(z + d == n - 1)
-            def _():
-                prepare(n - 1)
+            while behind < index:
+                columns_arrive(*steps[behind])
+                behind += 1
+        ready(d, k, prepare)
 
     for entry in steps[behind:]:
         columns_arrive(*entry)
@@ -282,22 +307,14 @@
             each_column(slab, k, False, sent)
 
 
-def product_kernel(sum_t_ref, dif_t_ref, cols_ref, weight_ref, scale_ref, inst_ref, lag_ref, plus, minus):
-    total, wide = plus.shape
-    for part in range(wide // LANES):
-        at = slice(part * LANES, (part + 1) * LANES)
-        c = cols_ref[0, :, at].astype(jnp.float32)
-        lagged = pltpu.roll(c, total - LAG, 0)
-        w = weight_ref[...]
-        plus[:, at] = (w * (c + lagged)).astype(jnp.bfloat16)
-        minus[:, at] = (w * (c - lagged)).astype(jnp.bfloat16)
+def product_kernel(sum_t_ref, dif_t_ref, plus_ref, minus_ref, scale_ref, inst_ref, lag_ref):
     height = sum_t_ref.shape[0]
     block = min(512, height)
     scale = scale_ref[0:1, 0:1]
     for index in range(height // block):
         at = slice(index * block, (index + 1) * block)
-        a = jnp.dot(sum_t_ref[at, :], plus[...], preferred_element_type=jnp.float32)
-        b = jnp.dot(dif_t_ref[at, :], minus[...], preferred_element_type=jnp.float32)
+        a = jnp.dot(sum_t_ref[at, :], plus_ref[0], preferred_element_type=jnp.float32)
+        b = jnp.dot(dif_t_ref[at, :], minus_ref[0], preferred_element_type=jnp.float32)
         inst_ref[at, :] = (a + b) * scale
         lag_ref[at, :] = (a - b) * scale
 
@@ -311,19 +328,21 @@
     seg = jnp.broadcast_to(segment_ids[None, :], (8, slab_rows))
     vmem = pl.BlockSpec(memory_space=pltpu.VMEM)
     dma = pltpu.SemaphoreType.DMA
-    sum_t, dif_t, cols, weight, scale = pl.pallas_call(
+    sum_t, dif_t, plus, minus, scale = pl.pallas_call(
         functools.partial(gather_kernel, n, tiles, pc),
         out_shape=(
             jax.ShapeDtypeStruct((width, total), jnp.bfloat16),
             jax.ShapeDtypeStruct((width, total), jnp.bfloat16),
             jax.ShapeDtypeStruct((pc, total, width), jnp.bfloat16),
-            jax.ShapeDtypeStruct((total, LANES), jnp.float32),
+            jax.ShapeDtypeStruct((pc, total, width), jnp.bfloat16),
             jax.ShapeDtypeStruct((8, LANES), jnp.float32),
         ),
         in_specs=[vmem, vmem],
-        out_specs=(vmem, vmem, pl.BlockSpec(memory_space=pl.ANY), vmem, vmem),
+        out_specs=(vmem, vmem, vmem, vmem, vmem),
         scratch_shapes=[
             pltpu.VMEM((total + LANES, width), jnp.bfloat16),
+            pltpu.VMEM((pc, total + LANES, width), jnp.bfloat16),
+            pltpu.VMEM((total, LANES), jnp.float32),
             pltpu.VMEM((n, 8, slab_rows), jnp.int32),
             pltpu.VMEM((n, 8, slab_rows), jnp.float32),
             pltpu.VMEM((n, sum_rows, LANES), jnp.float32),
@@ -333,7 +352,7 @@
             dma((pc, n, PIECES)), dma((pc, n, PIECES)),
         ],
         compiler_params=pltpu.CompilerParams(
-            collective_id=0, has_side_effects=True, vmem_limit_bytes=44 * 1024 * 1024
+            collective_id=0, has_side_effects=True, vmem_limit_bytes=28 * 1024 * 1024
         ),
     )(frames, seg)
 
@@ -341,6 +360,7 @@
     per_tile = width // wide
     out = jax.ShapeDtypeStruct((width, pc * width), jnp.float32)
     whole = pl.BlockSpec((width, total), lambda j: (0, 0))
+    block = pl.BlockSpec((1, total, wide), lambda j: (j // per_tile, 0, j % per_tile))
     tile = pl.BlockSpec((width, wide), lambda j: (0, j))
     return pl.pallas_call(
         product_kernel,
@@ -348,19 +368,17 @@
         out_shape=(out, out),
         in_specs=[
             whole, whole,
-            pl.BlockSpec((1, total, wide), lambda j: (j // per_tile, 0, j % per_tile)),
-            pl.BlockSpec((total, LANES), lambda j: (0, 0)),
+            block, block,
             pl.BlockSpec((8, LANES), lambda j: (0, 0)),
         ],
         out_specs=(tile, tile),
-        scratch_shapes=[pltpu.VMEM((total, wide), jnp.bfloat16)] * 2,
-        compiler_params=pltpu.CompilerParams(vmem_limit_bytes=44 * 1024 * 1024),
+        compiler_params=pltpu.CompilerParams(vmem_limit_bytes=36 * 1024 * 1024),
         cost_estimate=pl.CostEstimate(
             flops=4 * total * width * width * pc,
             bytes_accessed=8 * width * width * pc + 6 * total * width,
             transcendentals=0,
         ),
-    )(sum_t, dif_t, cols, weight, scale)
+    )(sum_t, dif_t, plus, minus, scale)
 
 
 def solution(mesh):

time: 121 us -> 114 us (0.942)
  Pallas kernels: 115 us -> 110 us
  local copies, waits for them, and re-layouts: 4.45 us -> 2.27 us
    pallas_call x1, Pallas kernels: 91.8 us -> 87.9 us  [body(): pl.pallas_call(functools.partial(gather_kernel, n, tiles, pc), out_shape=...]
    unnamed x4 -> x2, local copies, waits for them, and re-layouts: 3.77 us -> 1.59 us
where the time goes in v3:
time: 114 us; the launch traced here: 113 us
  Pallas kernels  110 us (96%)
  local copies, waits for them, and re-layouts  2.27 us (2%)
    pallas_call x1, Pallas kernels, body(): pl.pallas_call(functools.partial(gather_kernel, n, tiles, pc), out_shape=...  87.9 us
    pallas_call x1, Pallas kernels, body(): pl.pallas_call(product_kernel, grid=(pc * per_tile,), out_shape=(out, out...  22.6 us

profile of v3, /device:TPU:3, one launch (start us, length us, event | category | flops | bytes accessed | tf_op | source)
XLA Modules:
  0.0 113.3 jit_solution(13558394747099555701)
XLA Ops:
  0.6 0.7 broadcast_in_dim.2.seg_ref
  1.3 0.0 copy-start
  1.3 1.6 %copy-done = f32[256,2048]{1,0:T(8,128)S(1)} copy-done((f32[256,2048]{1,0:T(8,128)S(1)}, f32[256,2048]{1,0:T(8,128)}, u32[]{:S(2)}) %copy-start) | copy-done | bytes 2097176
  2.9 87.9 %shard_map.41 = (bf16[2048,1024]{1,0:T(8,128)(2,1)S(1)}, bf16[2048,1024]{1,0:T(8,128)(2,1)S(1)}, bf16[1,1024,2048]{2,1,0:T(8,128)(2,1)S(1)}, bf16[1,1024,2048]{2,1,0:T(8,128)(2,1)S(1)}, f32[8,128]{1,0:T(8,128)S(1)}) custom-call(f32[256,2048]{1,0:T(8,128)S(1)} %copy-done, s32[8,256]{1,0:T(8,128)S(1)} %broadcast_in_dim.2.seg_ref), custom_call_target="tpu_custom_call" | custom-call | tf_op jit(solution)/shard_map/pallas_call | solution.py:331
  90.8 22.6 %shard_map.42 = (f32[2048,2048]{1,0:T(8,128)}, f32[2048,2048]{1,0:T(8,128)}) custom-call(bf16[2048,1024]{1,0:T(8,128)(2,1)S(1)} %get-tuple-element.7.sum_t_ref, bf16[2048,1024]{1,0:T(8,128)(2,1)S(1)} %get-tuple-element.8.dif_t_ref, bf16[1,1024,2048]{2,1,0:T(8,128)(2,1)S(1)} %get-tuple-element.9.plus_ref, ...), custom_call_target="tpu_custom_call" | custom-call | flops 17179869184 | bytes 46137344 | tf_op jit(solution)/shard_map/pallas_call | solution.py:365
Async XLA Ops:
  1.3 1.6 %copy-start = (f32[256,2048]{1,0:T(8,128)S(1)}, f32[256,2048]{1,0:T(8,128)}, u32[]{:S(2)}) copy-start(f32[256,2048]{1,0:T(8,128)} %frames_ref.1) | copy-start | bytes 6291460
